TPU v7x, 128 devices: a whole 4x4x4 slice. The times are simulated.
128 devices in a mesh: rows: 16 (over x, y), store: 8 (over z, core).
Axes of the slice: x: 4, y: 4, z: 4, core: 2. Of those that a mesh axis runs over, the one named last changes fastest.
Arguments:
- stored: float32 [128, 1048576], P('store', 'rows'), as said below
- snap_slot: int32 [64], replicated, may hold values from 0 to 127, as said below
Outputs:
- modes: float32 [64, 1048576], P(None, ('rows', 'store'))
- factor: float32 [64, 64], replicated
Inputs may be any that keep to these rules, and one draw needn't show every extreme that they name: `snap_slot`: the numbers are distinct slots; slots s * 16 to (s + 1) * 16 - 1 belong to storage owner s. Owners hold uneven numbers of the panel's snapshots; one owner holds exactly 16 of them. `stored`: entries are finite; the panel has full rank.
All inputs are finite; a program needn't handle non-finite values.
Results may differ from a plain program's by a relative error of at most 0.0003.
Values sent between devices are 32-bit elements; how exact they have to be, the bound alone decides.
No kernel may reach another device: no remote copies, remote signals or barrier semaphores. Data moves between devices by JAX's collectives and lax.ppermute only.
A program may use at most 128 MiB of HBM per device.

v0:
```python
import math

import jax
import jax.numpy as jnp
from jax import lax
from jax.experimental import pallas as pl
from jax.experimental.pallas import tpu as pltpu
from jax.sharding import PartitionSpec as P

HIGHEST = lax.Precision.HIGHEST
UP = 2.0**24


def dot(a, b):
    return jnp.dot(a, b, precision=HIGHEST, preferred_element_type=jnp.float32)


def iota(shape, dim):
    return lax.broadcasted_iota(jnp.int32, shape, dim)


def power_above(value):
    c, inverse = jnp.ones_like(value), jnp.ones_like(value)
    for e in (64, 32, 16, 8, 4, 2, 1):
        big = value * inverse > 2.0**e * 0.5
        c = jnp.where(big, c * 2.0**e, c)
        inverse = jnp.where(big, inverse * 2.0**-e, inverse)
    for e in (64, 32, 16, 8, 4, 2, 1):
        small = (value * inverse <= 2.0**-e) & (c > 2.0 ** (e - 126))
        c = jnp.where(small, c * 2.0**-e, c)
        inverse = jnp.where(small, inverse * 2.0**e, inverse)
    return c, inverse


def row_of(column):
    n = column.shape[0]
    return jnp.sum(jnp.where(iota((n, n), 0) == iota((n, n), 1), column, 0.0), axis=0, keepdims=True)


def two_sum(a, b):
    s = a + b
    t = s - a
    return s, (a - (s - t)) + (b - t)


def pair_add(first, second):
    s, e = two_sum(first[0], second[0])
    return s, (first[1] + second[1]) + e * UP


def nearest(x):
    return lax.round(x, lax.RoundingMethod.TO_NEAREST_EVEN)


def pieces(x, count):
    out = []
    t = x * 256.0
    for i in range(count):
        n = nearest(t)
        out.append(n)
        t = (t - n) * 512.0
    return out, t


def levels_to_pair(levels):
    hi, lo = levels[0], jnp.zeros_like(levels[0])
    for l in range(1, len(levels)):
        hi, e = two_sum(hi, levels[l] * 2.0 ** (-9 * l))
        lo = lo + e
    return two_sum(hi, lo)


def eliminate(gram, block=8):
    n = gram.shape[0]
    rows, columns = iota((n, n), 0), iota((n, n), 1)
    whole = jnp.concatenate([gram, (rows == columns).astype(jnp.float32)], axis=1)
    lane = iota((8, 2 * n), 1)
    sub = iota((8, 2 * n), 0)
    g = n // 8
    blocks = [whole[8 * i : 8 * i + 8] for i in range(g)]
    done = []
    for b in range(g):
        cols = {}
        for i in range(b, g):
            for q in range(8):
                j = 8 * b + q
                cols[i, q] = jnp.broadcast_to(blocks[i][:, j : j + 1], (8, 2 * n))
        mult = {}
        pivots = jnp.ones((8, 2 * n), jnp.float32)
        rowsb = blocks[b]

        def spread(value, q):
            return jnp.broadcast_to(value[q : q + 1], (8, 2 * n))

        for q in range(0, 8, 2):
            p, o, r = spread(cols[b, q], q), spread(cols[b, q + 1], q), spread(cols[b, q + 1], q + 1)
            determinant = p * r - o * o
            w, v = 1.0 / p, p * (1.0 / determinant)
            ratio = o * w
            for i in range(b, g):
                first = cols[i, q] * w
                second = (cols[i, q + 1] - cols[i, q] * ratio) * v
                if i == b:
                    first = jnp.where(sub > q, first, 0.0)
                    second = jnp.where(sub > q + 1, second, 0.0)
                mult[i, q], mult[i, q + 1] = first, second
            pivots = jnp.where(sub == q, p, jnp.where(sub == q + 1, r - o * ratio, pivots))
            row = spread(rowsb, q)
            rowsb = rowsb - mult[b, q] * row
            rowsb = rowsb - mult[b, q + 1] * spread(rowsb, q + 1)
            for c in range(q + 2, 8):
                a0 = spread(cols[b, c], q)
                a1 = spread(cols[b, c], q + 1) - ratio * a0
                for i in range(b, g):
                    cols[i, c] = (cols[i, c] - mult[i, q] * a0) - mult[i, q + 1] * a1
        for i in range(b + 1, g):
            value = blocks[i]
            for q in range(8):
                value = value - mult[i, q] * jnp.broadcast_to(rowsb[q : q + 1], (8, 2 * n))
            blocks[i] = value
        s = lax.rsqrt(pivots)
        s = s * (1.5 - 0.5 * pivots * s * s)
        done.append(rowsb * s)
    whole = jnp.concatenate(done, axis=0)
    upper = jnp.where(rows <= columns, whole[:, :n], 0.0)
    lower = jnp.where(rows >= columns, whole[:, n:], 0.0)
    return upper, lower


def bf16_dot(a, b):
    return lax.dot_general(a, b, (((1,), (0,)), ((), ())), preferred_element_type=jnp.float32)


def wide_product(left, right, keep):
    n = left[0].shape[0]
    na, nb = len(left), len(right)
    l = jnp.concatenate([x.astype(jnp.bfloat16) for x in left], axis=0)
    r = jnp.concatenate([x.astype(jnp.bfloat16) for x in right], axis=1)
    m = bf16_dot(l, r)
    out = []
    for lev in range(keep):
        acc = None
        for a in range(na):
            c = lev - a
            if 0 <= c < nb:
                t = m[a * n : (a + 1) * n, c * n : (c + 1) * n]
                acc = t if acc is None else acc + t
        out.append(acc)
    return out


def second_gram(hi, lo, lower):
    first, rest = pieces(hi, 3)
    rest = rest + lo * (2.0 ** (8 + 27) / UP)
    out = []
    for _ in range(3):
        n = nearest(rest)
        out.append(n)
        rest = (rest - n) * 512.0
    g = first + out
    top = jnp.max(jnp.abs(lower), axis=1, keepdims=True)
    u, v = power_above(top)
    ls, _ = pieces(lower * v, 4)
    lt = [x.T for x in ls]
    ur = row_of(u)
    lev = wide_product(g, lt, 7)
    ch, cl = levels_to_pair(lev)
    scale = ur * 2.0**-16
    ch, cl = ch * scale, cl * scale
    cs, rest = pieces(ch * 0.5, 3)
    rest = rest + cl * (0.5 * 2.0 ** (8 + 27))
    for _ in range(2):
        n = nearest(rest)
        cs.append(n)
        rest = (rest - n) * 512.0
    lev = wide_product(ls, cs, 7)
    h, l = levels_to_pair(lev)
    return (h + l) * (u * 2.0**-15)


def finish(hi, lo, count):
    n = hi.shape[0]
    eye = iota((n, n), 0) == iota((n, n), 1)
    diag = jnp.sum(jnp.where(eye, hi, 0.0), axis=1, keepdims=True)
    d, di = power_above(jnp.sqrt(diag))
    dr, dir_ = row_of(d), row_of(di)
    hs = (hi * di) * dir_
    ls = (lo * di) * dir_
    r1, l1 = eliminate(hs)
    g2 = second_gram(hs, ls, l1)
    r2, l2 = eliminate(g2)
    scale = math.sqrt(count)
    w = dot(l2, l1) * (dir_ * scale)
    factor = dot(r2, r1) * (dr * (1.0 / scale))
    return w, factor, g2


def combine(acc, c):
    n = acc.shape[0] // 3
    cr = row_of(c)
    part = [[acc[a * n : (a + 1) * n, b * n : (b + 1) * n] for b in range(4)] for a in range(3)]
    levels = []
    for lev in range(6):
        total = None
        for a in range(3):
            b = lev - a
            if 0 <= b < 4:
                x = part[a][b] + part[a][b].T if b == 3 else part[a][b]
                total = x if total is None else total + x
        levels.append(total)
    hi = jnp.zeros((n, n), jnp.float32)
    lo = jnp.zeros((n, n), jnp.float32)
    for lev, t in enumerate(levels):
        high = lax.shift_right_arithmetic(t, 14)
        low = (t - lax.shift_left(high, 14)).astype(jnp.float32) * 2.0 ** (-9 * lev)
        high = high.astype(jnp.float32) * 2.0 ** (14 - 9 * lev)
        hi, e = two_sum(hi, high)
        lo = lo + e
        hi, e = two_sum(hi, low)
        lo = lo + e
    hi, lo = two_sum(hi, lo)
    f = 2.0**-16
    return ((hi * f) * c) * cr, (((lo * (f * UP)) * c) * cr)


STEP = 256
CORES = 2
QUARTERS = 4
BIG = pltpu.CompilerParams(vmem_limit_bytes=8 * 2**20)
ANY = pl.BlockSpec(memory_space=pl.ANY)
HBM = pl.BlockSpec(memory_space=pltpu.HBM)
VMEM = pl.BlockSpec(memory_space=pltpu.VMEM)


def each(count, rolled, body, carry):
    if rolled:
        return lax.fori_loop(0, count, body, carry)
    for i in range(count):
        carry = body(i, carry)
    return carry


def columns_at(start):
    return pl.ds(start if isinstance(start, int) else pl.multiple_of(start, STEP), STEP)


def thirds(x):
    high = x.astype(jnp.bfloat16)
    rest = x - high.astype(jnp.float32)
    mid = rest.astype(jnp.bfloat16)
    low = (rest - mid.astype(jnp.float32)).astype(jnp.bfloat16)
    return jnp.concatenate([high, mid, low], axis=0)


def place():
    store = lax.axis_index("store")
    return store // CORES, store % CORES


def row_sum(mask_value):
    return jnp.sum(mask_value, axis=0, keepdims=True)


def positions(slot, span):
    n = slot.shape[1]
    column = jnp.sum(jnp.where(iota((n, n), 0) == iota((n, n), 1), slot, 0), axis=1, keepdims=True)
    before = (column < slot) & (column // span == slot // span)
    return slot // span, row_sum(before.astype(jnp.int32))


def part_kernel(distance, chips, stored_ref, out_ref, sem):
    columns = out_ref.shape[1]
    z, core = place()
    owner = lax.rem(z + distance, chips) * CORES + 1 - core
    start = pl.multiple_of(owner * columns, columns)
    copy = pltpu.make_async_copy(stored_ref.at[:, pl.ds(start, columns)], out_ref, sem)
    copy.start()
    copy.wait()


def pick_kernel(distance, passed, index, chips, capacity, *refs):
    stored_ref, slot_ref, other_ref = refs[:3]
    sems = refs[-1]
    slots, columns = other_ref.shape[-2:]
    z, core = place()

    def part(d, c):
        owner = lax.rem(z + d, chips) * CORES + c
        return stored_ref.at[:, pl.ds(pl.multiple_of(owner * columns, columns), columns)]

    copies = []
    if passed:
        out, parts_ref, own_ref, held_ref = refs[-5:-1]
        copies.append(pltpu.make_async_copy(part(distance, core), own_ref, sems.at[0]))
        for i, d in enumerate(passed):
            copies.append(pltpu.make_async_copy(part(d, 1 - core), held_ref.at[i], sems.at[1 + i]))
    else:
        out, own_ref, got_ref = refs[-4:-1]
        copies.append(pltpu.make_async_copy(part(distance, core), own_ref, sems.at[0]))
        copies.append(pltpu.make_async_copy(other_ref.at[index], got_ref, sems.at[1]))
        other_ref = got_ref
    for copy in copies:
        copy.start()
    slot = slot_ref[...]
    span = CORES * slots
    chip, position = positions(slot, span)
    local = slot - (chip * CORES + core) * slots
    local = jnp.where(local < 0, local + span, local)
    count = slot.shape[1]
    rows = QUARTERS * capacity
    row, column = iota((rows, count), 0), iota((span, count), 0)
    quarter = sum((row >= q * capacity).astype(jnp.int32) for q in range(1, QUARTERS))
    ranks = ((chip == z) & (position == row - quarter * capacity)).astype(jnp.bfloat16)
    locals_ = (local == column).astype(jnp.bfloat16)
    locals_ = jnp.concatenate([locals_] * QUARTERS, axis=0)
    hit = lax.dot_general(ranks, locals_, (((1,), (1,)), ((), ())), preferred_element_type=jnp.float32)
    shape = (rows, QUARTERS * span)
    quarter = sum((iota(shape, 0) >= q * capacity).astype(jnp.int32) for q in range(1, QUARTERS))
    selector = jnp.where(quarter == iota(shape, 1) // span, hit, 0.0).astype(jnp.bfloat16)
    selector = jnp.concatenate([selector] * 3, axis=1)
    wide = out.shape[1]

    def step(i, carry):
        at = [columns_at(q * wide + i * STEP) for q in range(QUARTERS)]
        both = [ref[:, part] for part in at for ref in (own_ref, other_ref)]
        out[:, columns_at(i * STEP)] = bf16_dot(selector, thirds(jnp.concatenate(both, axis=0)))
        return carry

    if not passed:
        for copy in copies:
            copy.wait()
        each(wide // STEP, True, step, 0)
        return
    copies[0].wait()
    half = wide // STEP // 2
    each(half, False, step, 0)
    ends = []
    for i in range(len(passed)):
        copies[1 + i].wait()
        ends.append(pltpu.make_async_copy(held_ref.at[i], parts_ref.at[i], sems.at[1 + i]))
        ends[-1].start()
    each(wide // STEP - half, False, lambda i, carry: step(half + i, carry), 0)
    for end in ends:
        end.wait()


def picked(distance, chips, capacity, stored, slot, others, index, *after):
    _, slots, columns = others.shape
    return pl.pallas_call(
        lambda *refs: pick_kernel(distance, (), index, chips, capacity, *refs),
        out_shape=float_array(QUARTERS * capacity, columns // QUARTERS),
        in_specs=[HBM, VMEM, ANY] + [ANY] * len(after),
        scratch_shapes=[pltpu.VMEM((slots, columns), jnp.float32)] * 2 + [pltpu.SemaphoreType.DMA((2,))],
        compiler_params=BIG,
    )(stored, slot, others, *after)


def picked_first(distance, passed, chips, capacity, stored, slot, other):
    slots, columns = other.shape
    count = len(passed)
    return pl.pallas_call(
        lambda *refs: pick_kernel(distance, passed, None, chips, capacity, *refs),
        out_shape=(float_array(QUARTERS * capacity, columns // QUARTERS), float_array(count, slots, columns)),
        in_specs=[HBM, VMEM, VMEM],
        out_specs=(VMEM, ANY),
        scratch_shapes=[
            pltpu.VMEM((slots, columns), jnp.float32),
            pltpu.VMEM((count, slots, columns), jnp.float32),
            pltpu.SemaphoreType.DMA((1 + count,)),
        ],
        compiler_params=BIG,
    )(stored, slot, other)


def swap(part):
    return lax.ppermute(part, "store", [(i, i ^ 1) for i in range(lax.axis_size("store"))])


def send(block, d):
    store = lax.axis_size("store")
    return lax.ppermute(block, "store", [(i, (i + d * CORES) % store) for i in range(store)])


def ordered(parts, selector):
    return bf16_dot(selector, thirds(jnp.concatenate(parts, axis=0)))


def order_kernel(*refs):
    block_refs, selector_ref, out_ref = refs[:-2], refs[-2], refs[-1]
    selector = selector_ref[...]

    def step(i, carry):
        part = columns_at(i * STEP)
        out_ref[:, part] = ordered([ref[:, part] for ref in block_refs], selector)
        return carry

    each(out_ref.shape[1] // STEP, True, step, 0)


def gram_kernel(rolled, *refs):
    first_ref, second_ref, selector_ref, ready_ref, panel_ref, out_ref, held_ref, panel_held, sum_ref, sems = refs
    n, columns = panel_ref.shape
    wide = columns // QUARTERS

    fetches = []
    for j, ref in enumerate((first_ref, second_ref)):
        fetches.append(pltpu.make_async_copy(ref, held_ref.at[j], sems.at[0, j]))
        fetches[-1].start()
    selector = selector_ref[...]

    for fetch in fetches:
        fetch.wait()

    def gather(i, top):
        part = columns_at(i * STEP)
        got = ordered([held_ref[0, :, part], held_ref[1, :, part]], selector) + ready_ref[:, part]
        for q in range(QUARTERS):
            rows = got[q * n : (q + 1) * n]
            panel_held[:, columns_at(q * wide + i * STEP)] = rows
            top = jnp.maximum(top, jnp.abs(rows))
        return top

    top = each(wide // STEP, rolled, gather, jnp.zeros((n, STEP), jnp.float32))
    copies = []
    for q in range(QUARTERS):
        part = pl.ds(q * wide, wide)
        copies.append(pltpu.make_async_copy(panel_held.at[:, part], panel_ref.at[:, part], sems.at[1, q]))
        copies[-1].start()
    c, inverse = power_above(jnp.max(top, axis=1, keepdims=True))
    sum_ref[...] = jnp.zeros_like(sum_ref)

    def step(i, carry):
        parts, _ = pieces(panel_held[:, columns_at(i * STEP)] * inverse, 4)
        x = jnp.concatenate([p.astype(jnp.bfloat16) for p in parts], axis=0)
        h = lax.dot_general(x[: 3 * n], x, (((1,), (1,)), ((), ())), preferred_element_type=jnp.float32)
        sum_ref[...] += h.astype(jnp.int32)
        return carry

    each(columns // STEP, rolled, step, 0)
    packed = pack(*combine(sum_ref[...], c))
    for i in range(out_ref.shape[0]):
        out_ref[i] = packed
    for copy in copies:
        copy.wait()


def pack(hi, lo):
    h = hi.shape[0] // 2
    rows, columns = iota((h, h), 0), iota((h, h), 1)
    wide, diagonals = [], []
    for x in (hi, lo):
        a, b, c = x[:h, :h], x[:h, h:], x[h:, h:]
        diagonal = jnp.sum(jnp.where(rows == columns, c, 0.0), axis=0, keepdims=True)
        wide += [jnp.where(columns >= rows, a, c), b]
        diagonals += [diagonal, jnp.zeros_like(diagonal)]
    tail = jnp.broadcast_to(jnp.concatenate(diagonals, axis=1), (8, 4 * h))
    return jnp.concatenate([jnp.concatenate(wide, axis=1), tail], axis=0)


def unpack(packed):
    h = packed.shape[1] // 4
    rows, columns = iota((h, h), 0), iota((h, h), 1)
    main = packed[:h]
    turned = main.T
    out = []
    for i in (0, 2 * h):
        m, mt = main[:, i : i + h], turned[i : i + h]
        b, bt = main[:, i + h : i + 2 * h], turned[i + h : i + 2 * h]
        a = jnp.where(columns >= rows, m, mt)
        c = jnp.where(columns < rows, m, jnp.where(columns > rows, mt, packed[h : h + 1, i : i + h]))
        out.append(jnp.concatenate([jnp.concatenate([a, b], axis=1), jnp.concatenate([bt, c], axis=1)], axis=0))
    return out


def pair_sum(ref):
    half = ref.shape[2] // 2
    terms = [(ref[i], None) for i in range(ref.shape[0])]
    while len(terms) > 1:
        merged = []
        for (x, a), (y, b) in zip(terms[::2], terms[1::2]):
            total, e = two_sum(x, y)
            merged.append((total, e if a is None else (a + b) + e))
        terms = merged
    total, rest = terms[0]
    rest = jnp.where(iota(total.shape, 1) < half, rest * UP, 0.0)
    return total + pltpu.roll(rest, half, 1)


def sum_kernel(in_ref, out_ref):
    total = pair_sum(in_ref)
    for i in range(out_ref.shape[0]):
        out_ref[i] = total


def modes_kernel(count, pairs_ref, panel_ref, out_ref, factor_ref, panel_held, out_held, sems):
    fetch = pltpu.make_async_copy(panel_ref, panel_held, sems.at[sems.shape[0] - 1])
    fetch.start()
    weights, factor, _ = finish(*unpack(pair_sum(pairs_ref)), count)
    factor_ref[...] = factor
    n = weights.shape[0]
    w = thirds(weights)
    first, second, third = w[:n], w[n : 2 * n], w[2 * n :]
    none = jnp.zeros_like(first)
    left = jnp.concatenate(
        [
            jnp.concatenate([first, first, first], axis=1),
            jnp.concatenate([second, second, none], axis=1),
            jnp.concatenate([third, none, none], axis=1),
        ],
        axis=0,
    )
    fetch.wait()
    chunks = sems.shape[0] - 1
    wide = out_ref.shape[1] // chunks
    copies = []
    for i in range(chunks):
        for k in range(i * wide, (i + 1) * wide, STEP):
            got = bf16_dot(left, thirds(panel_held[:, k : k + STEP]))
            out_held[:, k : k + STEP] = (got[2 * n :] + got[n : 2 * n]) + got[:n]
        part = pl.ds(i * wide, wide)
        copies.append(pltpu.make_async_copy(out_held.at[:, part], out_ref.at[:, part], sems.at[i]))
        copies[-1].start()
    for copy in copies:
        copy.wait()


def float_array(*shape):
    return jax.ShapeDtypeStruct(shape, jnp.float32)


def relayout(capacity, stored, slot, other, chip, position):
    n = chip.shape[0]
    store = lax.axis_size("store")
    chips, columns = store // CORES, other.shape[1]
    z, _ = place()
    far, near = chips // 2, (1, chips - 1)
    rest = (*near, 0)
    block, parts = picked_first(far, rest, chips, capacity, stored, slot, other)
    blocks = {far: send(block, far)}
    others = swap(parts)
    for i, d in enumerate(rest):
        block = picked(d, chips, capacity, stored, slot, others, i, block)
        blocks[d] = send(block, d) if d else block
    distance = lax.rem(z - chip + chips, chips)
    first, last = (0, far), near

    def selector(distances):
        source = sum(jnp.where(distance == d, i + 1, 0) for i, d in enumerate(distances)) - 1
        source = jnp.where(source < 0, -(QUARTERS * capacity), source * QUARTERS * capacity + position)
        source = source[None, :] + jnp.arange(QUARTERS)[:, None] * capacity
        hit = source.reshape(-1)[:, None] == jnp.arange(len(distances) * QUARTERS * capacity)[None, :]
        return jnp.tile(hit.astype(jnp.bfloat16), (1, 3))

    ready = pl.pallas_call(
        order_kernel,
        out_shape=float_array(QUARTERS * n, columns // QUARTERS),
        compiler_params=BIG,
    )(*[blocks[d] for d in first], selector(first))
    shape = blocks[near[0]].shape
    return pl.pallas_call(
        lambda *refs: gram_kernel(capacity == CORES * stored.shape[0], *refs),
        out_shape=(float_array(n, columns), float_array(store, n // 2 + 8, 2 * n)),
        in_specs=[ANY, ANY, VMEM, VMEM],
        out_specs=(ANY, VMEM),
        scratch_shapes=[
            pltpu.VMEM((2, *shape), jnp.float32),
            pltpu.VMEM((n, columns), jnp.float32),
            pltpu.VMEM((3 * n, 4 * n), jnp.int32),
            pltpu.SemaphoreType.DMA((2, QUARTERS)),
        ],
        compiler_params=BIG,
    )(*[blocks[d] for d in last], selector(last), ready)


def per_device(stored, snap_slot):
    n = snap_slot.shape[0]
    slots = stored.shape[0]
    store, rows = lax.axis_size("store"), lax.axis_size("rows")
    columns, chips = stored.shape[1] // store, store // CORES
    part = pl.pallas_call(
        lambda *refs: part_kernel(chips // 2, chips, *refs),
        out_shape=float_array(slots, columns),
        in_specs=[HBM],
        scratch_shapes=[pltpu.SemaphoreType.DMA(())],
        compiler_params=BIG,
    )(stored)
    other = swap(part)
    chip = snap_slot // (slots * CORES)
    same = chip[:, None] == chip[None, :]
    position = jnp.sum((same & (snap_slot[None, :] < snap_slot[:, None])).astype(jnp.int32), axis=1)
    most = jnp.max(position) + 1
    capacities = (22, 24, 26, 32)
    choice = sum((most > c).astype(jnp.int32) for c in capacities[:-1])
    branches = [lambda *args, c=c: relayout(c, *args) for c in capacities]
    panel, pairs = lax.switch(choice, branches, stored, snap_slot[None, :], other, chip, position)
    pairs = lax.optimization_barrier(pairs)
    pairs = lax.all_to_all(pairs, "store", split_axis=0, concat_axis=0, tiled=True)
    pairs = pl.pallas_call(sum_kernel, out_shape=float_array(rows, *pairs.shape[1:]), compiler_params=BIG)(pairs)
    pairs = lax.all_to_all(pairs, "rows", split_axis=0, concat_axis=0, tiled=True)
    modes, factor = pl.pallas_call(
        lambda *refs: modes_kernel(columns * store * rows, *refs),
        out_shape=(float_array(n, columns), float_array(n, n)),
        in_specs=[VMEM, ANY],
        out_specs=(ANY, VMEM),
        scratch_shapes=[pltpu.VMEM((n, columns), jnp.float32)] * 2 + [pltpu.SemaphoreType.DMA((9,))],
        compiler_params=BIG,
    )(pairs, panel)
    return (modes, factor)


def solution(mesh):
    in_specs = (P("store", "rows"), P())
    out_specs = (P(None, ("rows", "store")), P())
    return jax.shard_map(
        per_device, mesh=mesh, in_specs=in_specs, out_specs=out_specs, check_vma=False
    )
```

profile of v0, /device:TPU:0, one launch (start us, length us, event | category | flops | bytes accessed | tf_op | source)
XLA Modules:
  0.0 87.0 jit_solution(9316308957545013597)
XLA Ops:
  0.6 0.0 copy-start.8
  0.6 1.1 %shard_map.41 = f32[16,8192]{1,0:T(8,128)S(1)} custom-call(f32[16,65536]{1,0:T(8,128)} %refs_0_.1), custom_call_target="tpu_custom_call" | custom-call | tf_op jit(solution)/shard_map/pallas_call | solution.py:580
  1.7 0.1 collective-permute-start.16
  1.8 0.0 copy-done.8
  1.8 0.2 convert_reduce_fusion
  2.0 0.6 reduce_max.9
  3.3 0.4 collective-permute-done.16
  3.7 48.7 %conditional.1 = ((f32[64,8192]{1,0:T(8,128)S(1)}, f32[8,40,128]{2,1,0:T(8,128)S(1)})) conditional(s32[]{:T(128)} %clamp.3, (f32[16,65536]{1,0:T(8,128)}, s32[1,64]{1,0:T(1,128)S(1)}, f32[16,8192]{1,0:T(8,128)S(1)}, s32[64]{0:T(128)S(1)}, s32[64]{0:T(128)S(1)}) %tuple.36, (f32[16,65536]{1,0:T(8,128)}, ...), branch_computations={%region_2.3_spmd, %region_3.4_spmd, %region_4.5_spmd, %region_5.6_... | conditional | flops 264469 | bytes 38546060 | solution.py:595
  3.7 2.8 %branch_1_fun.6 = (f32[96,2048]{1,0:T(8,128)}, f32[3,16,8192]{2,1,0:T(8,128)S(1)}) custom-call(f32[16,65536]{1,0:T(8,128)} %get-tuple-element.47.refs_0_, s32[1,64]{1,0:T(1,128)S(1)} %get-tuple-element.48.refs_1_, f32[16,8192]{1,0:T(8,128)S(1)} %get-tuple-element.49.refs_2_), custom_call_target="tpu_custom_call" | custom-call | tf_op jit(solution)/shard_map/cond/branch_1_fun/pallas_call | solution.py:361
  6.5 0.2 collective-permute-start.4
  6.7 4.0 %collective-permute-start.7 = (f32[96,2048]{1,0:T(8,128)}, f32[96,2048]{1,0:T(8,128)}, u32[]{:S(2)}, u32[]{:S(2)}) collective-permute-start(f32[96,2048]{1,0:T(8,128)} %get-tuple-element.51.refs_3_), channel_id=1, source_target_pairs={{0,4},{1,5},{2,6},{3,7},{4,0},{5,1},{6,2},{7,3},{8,12},{9,13},{10,... | collective-permute-start | bytes 2359304 | tf_op jit(solution)/shard_map/cond/branch_1_fun/ppermute | solution.py:381
  10.7 0.0 copy-start.5
  10.8 0.0 collective-permute-done.4.refs_2_
  10.8 2.7 %branch_1_fun.7.refs_3_ = f32[96,2048]{1,0:T(8,128)S(1)} custom-call(f32[16,65536]{1,0:T(8,128)} %get-tuple-element.47.refs_0_, s32[1,64]{1,0:T(1,128)S(1)} %get-tuple-element.48.refs_1_, f32[3,16,8192]{2,1,0:T(8,128)S(1)} %collective-permute-done.4.refs_2_, f32[96,2048]{1,0:T(8,128)} %get-tuple-element.51.refs_3_), custom_call_target="tpu_custom_call" | custom-call | tf_op jit(solution)/shard_map/cond/branch_1_fun/pallas_call | solution.py:349
  13.5 1.3 %collective-permute-start.5 = (f32[96,2048]{1,0:T(8,128)S(1)}, f32[96,2048]{1,0:T(8,128)}, u32[]{:S(2)}, u32[]{:S(2)}) collective-permute-start(f32[96,2048]{1,0:T(8,128)S(1)} %branch_1_fun.7.refs_3_), channel_id=1, source_target_pairs={{0,2},{1,3},{2,4},{3,5},{4,6},{5,7},{6,0},{7,1},{8,10},{9,11},{10,... | collective-permute-start | bytes 2359304 | tf_op jit(solution)/shard_map/cond/branch_1_fun/ppermute | solution.py:381
  14.8 0.0 copy-done.5
  14.8 1.8 %branch_1_fun.8.refs_3_ = f32[96,2048]{1,0:T(8,128)S(1)} custom-call(f32[16,65536]{1,0:T(8,128)S(1)} %copy-done.5, s32[1,64]{1,0:T(1,128)S(1)} %get-tuple-element.48.refs_1_, f32[3,16,8192]{2,1,0:T(8,128)S(1)} %collective-permute-done.4.refs_2_, f32[96,2048]{1,0:T(8,128)S(1)} %branch_1_fun.7.refs_3_), custom_call_target="tpu_custom_call" | custom-call | tf_op jit(solution)/shard_map/cond/branch_1_fun/pallas_call | solution.py:349
  16.6 2.3 %collective-permute-start.6 = (f32[96,2048]{1,0:T(8,128)S(1)}, f32[96,2048]{1,0:T(8,128)}, u32[]{:S(2)}, u32[]{:S(2)}) collective-permute-start(f32[96,2048]{1,0:T(8,128)S(1)} %branch_1_fun.8.refs_3_), channel_id=1, source_target_pairs={{0,6},{1,7},{2,0},{3,1},{4,2},{5,3},{6,4},{7,5},{8,14},{9,15},{10,... | collective-permute-start | bytes 2359304 | tf_op jit(solution)/shard_map/cond/branch_1_fun/ppermute | solution.py:381
  18.9 0.1 broadcast_add_fusion.2
  19.0 0.1 add.212
  19.1 0.9 %copy.14.refs_2_ = bf16[256,576]{1,0:T(8,128)(2,1)} copy(bf16[256,576]{0,1:T(8,128)(2,1)S(1)} %bitcast.13) | data formatting | bytes 589824 | tf_op jit(solution)/shard_map/cond/branch_1_fun/tile | solution.py:552
  20.0 0.1 add.206
  20.1 0.7 tile.40
  20.9 1.2 %copy.15.refs_2_ = bf16[256,576]{1,0:T(8,128)(2,1)S(1)} copy(bf16[256,576]{0,1:T(8,128)(2,1)} %bitcast.14) | data formatting | bytes 589824 | tf_op jit(solution)/shard_map/cond/branch_1_fun/tile | solution.py:552
  22.0 0.0 copy-start.3
  22.1 2.6 %branch_1_fun.9.refs_0_ = f32[96,2048]{1,0:T(8,128)S(1)} custom-call(f32[16,65536]{1,0:T(8,128)} %get-tuple-element.47.refs_0_, s32[1,64]{1,0:T(1,128)S(1)} %get-tuple-element.48.refs_1_, f32[3,16,8192]{2,1,0:T(8,128)S(1)} %collective-permute-done.4.refs_2_, f32[96,2048]{1,0:T(8,128)S(1)} %branch_1_fun.8.refs_3_), custom_call_target="tpu_custom_call" | custom-call | tf_op jit(solution)/shard_map/cond/branch_1_fun/pallas_call | solution.py:349
  24.7 4.8 %collective-permute-done.7.refs_1_ = f32[96,2048]{1,0:T(8,128)} collective-permute-done((f32[96,2048]{1,0:T(8,128)}, f32[96,2048]{1,0:T(8,128)}, u32[]{:S(2)}, u32[]{:S(2)}) %collective-permute-start.7) | collective-permute-done | bytes 786464 | tf_op jit(solution)/shard_map/cond/branch_1_fun/ppermute | solution.py:381
  29.5 0.0 copy-done.3
  29.5 3.4 %branch_1_fun.10.refs_3_ = f32[256,2048]{1,0:T(8,128)S(1)} custom-call(f32[96,2048]{1,0:T(8,128)S(1)} %branch_1_fun.9.refs_0_, f32[96,2048]{1,0:T(8,128)} %collective-permute-done.7.refs_1_, bf16[256,576]{1,0:T(8,128)(2,1)S(1)} %copy-done.3), custom_call_target="tpu_custom_call" | custom-call | tf_op jit(solution)/shard_map/cond/branch_1_fun/pallas_call | solution.py:554
  32.8 13.9 %collective-permute-done.6.refs_1_ = f32[96,2048]{1,0:T(8,128)} collective-permute-done((f32[96,2048]{1,0:T(8,128)S(1)}, f32[96,2048]{1,0:T(8,128)}, u32[]{:S(2)}, u32[]{:S(2)}) %collective-permute-start.6) | collective-permute-done | bytes 786464 | tf_op jit(solution)/shard_map/cond/branch_1_fun/ppermute | solution.py:381
  46.7 0.0 collective-permute-done.5.refs_0_
  46.7 5.5 %branch_1_fun.11 = (f32[64,8192]{1,0:T(8,128)S(1)}, f32[8,40,128]{2,1,0:T(8,128)S(1)}) custom-call(f32[96,2048]{1,0:T(8,128)} %collective-permute-done.5.refs_0_, f32[96,2048]{1,0:T(8,128)} %collective-permute-done.6.refs_1_, bf16[256,576]{1,0:T(8,128)(2,1)S(1)} %copy.15.refs_2_, f32[256,2048]{1,0:T(8,128)S(1)} %branch_1_fun.10.refs_3_), custom_call_target="tpu_custom_call" | custom-call | tf_op jit(solution)/shard_map/cond/branch_1_fun/pallas_call | solution.py:560
  52.4 10.2 %all_to_all.10.in_ref = f32[8,40,128]{2,1,0:T(8,128)S(1)} all-to-all(f32[8,40,128]{2,1,0:T(8,128)S(1)} %get-tuple-element.72), channel_id=1, replica_groups=mesh['rows'=16,'store'=8] {'store'}, dimensions={0} | all-to-all | bytes 327680 | tf_op jit(solution)/shard_map/all_to_all | solution.py:597
  62.6 0.1 shard_map.42
  62.7 15.8 %all_to_all.11.refs_0_ = f32[16,40,128]{2,1,0:T(8,128)S(1)} all-to-all(f32[16,40,128]{2,1,0:T(8,128)S(1)} %shard_map.42), channel_id=1, replica_groups=mesh['rows'=16,'store'=8] {'rows'}, dimensions={0} | all-to-all | bytes 655360 | tf_op jit(solution)/shard_map/all_to_all | solution.py:599
  78.5 8.3 %shard_map.43 = (f32[64,8192]{1,0:T(8,128)}, f32[64,64]{1,0:T(8,128)}) custom-call(f32[16,40,128]{2,1,0:T(8,128)S(1)} %all_to_all.11.refs_0_, f32[64,8192]{1,0:T(8,128)S(1)} %get-tuple-element.73.refs_1_), custom_call_target="tpu_custom_call" | custom-call | tf_op jit(solution)/shard_map/pallas_call | solution.py:600
  (7 shorter events, 0.1 us)
Async XLA Ops:
  0.6 1.2 %copy-start.8 = (s32[64]{0:T(128)S(1)}, s32[64]{0:T(128)}, u32[]{:S(2)}) copy-start(s32[64]{0:T(128)} %param.7) | copy-start | bytes 772
  1.7 2.0 %collective-permute-start.16 = (f32[16,8192]{1,0:T(8,128)S(1)}, f32[16,8192]{1,0:T(8,128)S(1)}, u32[]{:S(2)}, u32[]{:S(2)}) collective-permute-start(f32[16,8192]{1,0:T(8,128)S(1)} %shard_map.41), channel_id=1, source_target_pairs={{0,1},{1,0},{2,3},{3,2},{4,5},{5,4},{6,7},{7,6},{8,9},{9,8},{10,11... | collective-permute-start | bytes 1572872 | tf_op jit(solution)/shard_map/ppermute | solution.py:376
  6.5 4.2 %collective-permute-start.4 = (f32[3,16,8192]{2,1,0:T(8,128)S(1)}, f32[3,16,8192]{2,1,0:T(8,128)S(1)}, u32[]{:S(2)}, u32[]{:S(2)}) collective-permute-start(f32[3,16,8192]{2,1,0:T(8,128)S(1)} %get-tuple-element.50), channel_id=1, source_target_pairs={{0,1},{1,0},{2,3},{3,2},{4,5},{5,4},{6,7},{7,6},{8,9},{9,8},{10,11... | collective-permute-start | bytes 4718600 | tf_op jit(solution)/shard_map/cond/branch_1_fun/ppermute | solution.py:376
  6.7 22.7 %collective-permute-start.7 = (f32[96,2048]{1,0:T(8,128)}, f32[96,2048]{1,0:T(8,128)}, u32[]{:S(2)}, u32[]{:S(2)}) collective-permute-start(f32[96,2048]{1,0:T(8,128)} %get-tuple-element.51.refs_3_), channel_id=1, source_target_pairs={{0,4},{1,5},{2,6},{3,7},{4,0},{5,1},{6,2},{7,3},{8,12},{9,13},{10,... | collective-permute-start | bytes 2359304 | tf_op jit(solution)/shard_map/cond/branch_1_fun/ppermute | solution.py:381
  10.7 4.1 %copy-start.5 = (f32[16,65536]{1,0:T(8,128)S(1)}, f32[16,65536]{1,0:T(8,128)}, u32[]{:S(2)}) copy-start(f32[16,65536]{1,0:T(8,128)} %get-tuple-element.47.refs_0_) | copy-start | bytes 12582916 | tf_op jit(solution)/shard_map/cond
  13.5 33.2 %collective-permute-start.5 = (f32[96,2048]{1,0:T(8,128)S(1)}, f32[96,2048]{1,0:T(8,128)}, u32[]{:S(2)}, u32[]{:S(2)}) collective-permute-start(f32[96,2048]{1,0:T(8,128)S(1)} %branch_1_fun.7.refs_3_), channel_id=1, source_target_pairs={{0,2},{1,3},{2,4},{3,5},{4,6},{5,7},{6,0},{7,1},{8,10},{9,11},{10,... | collective-permute-start | bytes 2359304 | tf_op jit(solution)/shard_map/cond/branch_1_fun/ppermute | solution.py:381
  16.6 30.1 %collective-permute-start.6 = (f32[96,2048]{1,0:T(8,128)S(1)}, f32[96,2048]{1,0:T(8,128)}, u32[]{:S(2)}, u32[]{:S(2)}) collective-permute-start(f32[96,2048]{1,0:T(8,128)S(1)} %branch_1_fun.8.refs_3_), channel_id=1, source_target_pairs={{0,6},{1,7},{2,0},{3,1},{4,2},{5,3},{6,4},{7,5},{8,14},{9,15},{10,... | collective-permute-start | bytes 2359304 | tf_op jit(solution)/shard_map/cond/branch_1_fun/ppermute | solution.py:381
  22.0 7.4 %copy-start.3 = (bf16[256,576]{1,0:T(8,128)(2,1)S(1)}, bf16[256,576]{1,0:T(8,128)(2,1)}, u32[]{:S(2)}) copy-start(bf16[256,576]{1,0:T(8,128)(2,1)} %copy.14.refs_2_) | copy-start | bytes 884740 | tf_op jit(solution)/shard_map/cond
where the time goes:
time: 85.9 us; the launch traced here: 87 us
  Pallas kernels  28.3 us (33%)
  blocking collectives  25.9 us (30%)
  waiting for transfers between devices  19.1 us (22%)
  starting transfers between devices  7.84 us (9%)
  local copies, waits for them, and re-layouts  3 us (3%)
  between operations  1.54 us (2%)
  other arithmetic  0.98 us (1%)
    ppermute x3, waiting for transfers between devices, send(): lax.ppermute(block, 'store', [(i, (i + d * CORES) % store) for i in range...  18.7 us
    all_to_all x1, blocking collectives, per_device(): lax.all_to_all(pairs, 'rows', split_axis=0, concat_axis=0, tiled=True)  15.8 us
    all_to_all x1, blocking collectives, per_device(): lax.all_to_all(pairs, 'store', split_axis=0, concat_axis=0, tiled=True)  10.2 us
    pallas_call x1, Pallas kernels, per_device(): pl.pallas_call(lambda *refs: modes_kernel(columns * store * rows, *refs),...  8.28 us
    ppermute x3, starting transfers between devices, send(): lax.ppermute(block, 'store', [(i, (i + d * CORES) % store) for i in range...  7.54 us
    pallas_call x3, Pallas kernels, picked(): pl.pallas_call(lambda *refs: pick_kernel(distance, (), index, chips, capa...  7.17 us
    pallas_call x1, Pallas kernels, relayout(): pl.pallas_call(lambda *refs: gram_kernel(capacity == CORES * stored.shape...  5.47 us
    pallas_call x1, Pallas kernels, relayout(): pl.pallas_call(order_kernel, out_shape=float_array(QUARTERS * n, columns...  3.38 us
  transfers between devices with their start and end apart: 5, of which 3 were waited for; matrix products, arithmetic and copies ran while one was open for 5% of the time, Pallas kernels for 12%

commit v1 on v0

--- a/solution.py
+++ b/solution.py
@@ -1,3 +1,4 @@
+import functools
 import math
 
 import jax
@@ -226,6 +227,7 @@
 STEP = 256
 CORES = 2
 QUARTERS = 4
+HALVES = 2
 BIG = pltpu.CompilerParams(vmem_limit_bytes=8 * 2**20)
 ANY = pl.BlockSpec(memory_space=pl.ANY)
 HBM = pl.BlockSpec(memory_space=pltpu.HBM)
@@ -278,7 +280,7 @@
     copy.wait()
 
 
-def pick_kernel(distance, passed, index, chips, capacity, *refs):
+def pick_kernel(distance, passed, index, halves, chips, capacity, *refs):
     stored_ref, slot_ref, other_ref = refs[:3]
     sems = refs[-1]
     slots, columns = other_ref.shape[-2:]
@@ -290,15 +292,15 @@
 
     copies = []
     if passed:
-        out, parts_ref, own_ref, held_ref = refs[-5:-1]
+        out_ref, parts_ref, own_ref, got_ref, held_ref, made_ref = refs[-7:-1]
         copies.append(pltpu.make_async_copy(part(distance, core), own_ref, sems.at[0]))
+        copies.append(pltpu.make_async_copy(other_ref, got_ref, sems.at[1]))
         for i, d in enumerate(passed):
-            copies.append(pltpu.make_async_copy(part(d, 1 - core), held_ref.at[i], sems.at[1 + i]))
+            copies.append(pltpu.make_async_copy(part(d, 1 - core), held_ref.at[i], sems.at[2 + i]))
     else:
-        out, own_ref, got_ref = refs[-4:-1]
+        outs, (own_ref, got_ref) = refs[-3 - halves : -3], refs[-3:-1]
         copies.append(pltpu.make_async_copy(part(distance, core), own_ref, sems.at[0]))
         copies.append(pltpu.make_async_copy(other_ref.at[index], got_ref, sems.at[1]))
-        other_ref = got_ref
     for copy in copies:
         copy.start()
     slot = slot_ref[...]
@@ -318,37 +320,43 @@
     quarter = sum((iota(shape, 0) >= q * capacity).astype(jnp.int32) for q in range(1, QUARTERS))
     selector = jnp.where(quarter == iota(shape, 1) // span, hit, 0.0).astype(jnp.bfloat16)
     selector = jnp.concatenate([selector] * 3, axis=1)
-    wide = out.shape[1]
-
-    def step(i, carry):
-        at = [columns_at(q * wide + i * STEP) for q in range(QUARTERS)]
-        both = [ref[:, part] for part in at for ref in (own_ref, other_ref)]
+    wide = columns // QUARTERS
+
+    def step(out, first, i, carry):
+        at = [columns_at(q * wide + first + i * STEP) for q in range(QUARTERS)]
+        both = [ref[:, part] for part in at for ref in (own_ref, got_ref)]
         out[:, columns_at(i * STEP)] = bf16_dot(selector, thirds(jnp.concatenate(both, axis=0)))
         return carry
 
     if not passed:
         for copy in copies:
             copy.wait()
-        each(wide // STEP, True, step, 0)
+        for h, out in enumerate(outs):
+            each(out.shape[1] // STEP, True, functools.partial(step, out, h * out.shape[1]), 0)
         return
     copies[0].wait()
-    half = wide // STEP // 2
-    each(half, False, step, 0)
+    copies[1].wait()
+    half = wide // 2
     ends = []
-    for i in range(len(passed)):
-        copies[1 + i].wait()
-        ends.append(pltpu.make_async_copy(held_ref.at[i], parts_ref.at[i], sems.at[1 + i]))
+    for h in range(2):
+        part = pl.ds(h * half, half)
+        each(half // STEP, capacity == CORES * slots, functools.partial(step, made_ref.at[:, part], h * half), 0)
+        ends.append(pltpu.make_async_copy(made_ref.at[:, part], out_ref.at[:, part], sems.at[h]))
         ends[-1].start()
-    each(wide // STEP - half, False, lambda i, carry: step(half + i, carry), 0)
+        if h == 0:
+            for i in range(len(passed)):
+                copies[2 + i].wait()
+                ends.append(pltpu.make_async_copy(held_ref.at[i], parts_ref.at[i], sems.at[2 + i]))
+                ends[-1].start()
     for end in ends:
         end.wait()
 
 
-def picked(distance, chips, capacity, stored, slot, others, index, *after):
+def picked(distance, halves, chips, capacity, stored, slot, others, index, *after):
     _, slots, columns = others.shape
     return pl.pallas_call(
-        lambda *refs: pick_kernel(distance, (), index, chips, capacity, *refs),
-        out_shape=float_array(QUARTERS * capacity, columns // QUARTERS),
+        lambda *refs: pick_kernel(distance, (), index, halves, chips, capacity, *refs),
+        out_shape=(float_array(QUARTERS * capacity, columns // QUARTERS // halves),) * halves,
         in_specs=[HBM, VMEM, ANY] + [ANY] * len(after),
         scratch_shapes=[pltpu.VMEM((slots, columns), jnp.float32)] * 2 + [pltpu.SemaphoreType.DMA((2,))],
         compiler_params=BIG,
@@ -359,16 +367,18 @@
     slots, columns = other.shape
     count = len(passed)
     return pl.pallas_call(
-        lambda *refs: pick_kernel(distance, passed, None, chips, capacity, *refs),
+        lambda *refs: pick_kernel(distance, passed, None, 1, chips, capacity, *refs),
         out_shape=(float_array(QUARTERS * capacity, columns // QUARTERS), float_array(count, slots, columns)),
-        in_specs=[HBM, VMEM, VMEM],
-        out_specs=(VMEM, ANY),
+        in_specs=[HBM, VMEM, ANY],
+        out_specs=(ANY, ANY),
         scratch_shapes=[
             pltpu.VMEM((slots, columns), jnp.float32),
+            pltpu.VMEM((slots, columns), jnp.float32),
             pltpu.VMEM((count, slots, columns), jnp.float32),
-            pltpu.SemaphoreType.DMA((1 + count,)),
+            pltpu.VMEM((QUARTERS * capacity, columns // QUARTERS), jnp.float32),
+            pltpu.SemaphoreType.DMA((2 + count,)),
         ],
-        compiler_params=BIG,
+        compiler_params=pltpu.CompilerParams(vmem_limit_bytes=5 * 2**20),
     )(stored, slot, other)
 
 
@@ -385,20 +395,23 @@
     return bf16_dot(selector, thirds(jnp.concatenate(parts, axis=0)))
 
 
-def order_kernel(*refs):
-    block_refs, selector_ref, out_ref = refs[:-2], refs[-2], refs[-1]
+def order_kernel(blocks, *refs):
+    block_refs, selector_ref, ready_refs, out_ref = refs[:blocks], refs[blocks], refs[blocks + 1 : -1], refs[-1]
     selector = selector_ref[...]
 
     def step(i, carry):
         part = columns_at(i * STEP)
-        out_ref[:, part] = ordered([ref[:, part] for ref in block_refs], selector)
+        got = ordered([ref[:, part] for ref in block_refs], selector)
+        for ref in ready_refs:
+            got = got + ref[:, part]
+        out_ref[:, part] = got
         return carry
 
     each(out_ref.shape[1] // STEP, True, step, 0)
 
 
 def gram_kernel(rolled, *refs):
-    first_ref, second_ref, selector_ref, ready_ref, panel_ref, out_ref, held_ref, panel_held, sum_ref, sems = refs
+    first_ref, second_ref, selector_ref, done_ref, ready_ref, panel_ref, out_ref, held_ref, panel_held, sems = refs
     n, columns = panel_ref.shape
     wide = columns // QUARTERS
 
@@ -408,36 +421,41 @@
         fetches[-1].start()
     selector = selector_ref[...]
 
-    for fetch in fetches:
-        fetch.wait()
-
-    def gather(i, top):
-        part = columns_at(i * STEP)
-        got = ordered([held_ref[0, :, part], held_ref[1, :, part]], selector) + ready_ref[:, part]
+    blocks = wide // STEP
+    done = blocks // HALVES
+
+    def place_rows(i, got, top):
         for q in range(QUARTERS):
             rows = got[q * n : (q + 1) * n]
             panel_held[:, columns_at(q * wide + i * STEP)] = rows
             top = jnp.maximum(top, jnp.abs(rows))
         return top
 
-    top = each(wide // STEP, rolled, gather, jnp.zeros((n, STEP), jnp.float32))
+    def gather(i, top):
+        part = columns_at(i * STEP)
+        got = ordered([held_ref[0, :, part], held_ref[1, :, part]], selector)
+        return place_rows(done + i, got + ready_ref[:, columns_at((done + i) * STEP)], top)
+
+    top = jnp.zeros((n, STEP), jnp.float32)
+    top = each(done, rolled, lambda i, top: place_rows(i, done_ref[:, columns_at(i * STEP)], top), top)
+    for fetch in fetches:
+        fetch.wait()
+    top = each(blocks - done, rolled, gather, top)
     copies = []
     for q in range(QUARTERS):
         part = pl.ds(q * wide, wide)
         copies.append(pltpu.make_async_copy(panel_held.at[:, part], panel_ref.at[:, part], sems.at[1, q]))
         copies[-1].start()
     c, inverse = power_above(jnp.max(top, axis=1, keepdims=True))
-    sum_ref[...] = jnp.zeros_like(sum_ref)
 
     def step(i, carry):
         parts, _ = pieces(panel_held[:, columns_at(i * STEP)] * inverse, 4)
         x = jnp.concatenate([p.astype(jnp.bfloat16) for p in parts], axis=0)
         h = lax.dot_general(x[: 3 * n], x, (((1,), (1,)), ((), ())), preferred_element_type=jnp.float32)
-        sum_ref[...] += h.astype(jnp.int32)
-        return carry
-
-    each(columns // STEP, rolled, step, 0)
-    packed = pack(*combine(sum_ref[...], c))
+        return carry + h.astype(jnp.int32)
+
+    total = each(columns // STEP, rolled, step, jnp.zeros((3 * n, 4 * n), jnp.int32))
+    packed = pack(*combine(total, c))
     for i in range(out_ref.shape[0]):
         out_ref[i] = packed
     for copy in copies:
@@ -539,8 +557,9 @@
     blocks = {far: send(block, far)}
     others = swap(parts)
     for i, d in enumerate(rest):
-        block = picked(d, chips, capacity, stored, slot, others, i, block)
-        blocks[d] = send(block, d) if d else block
+        made = picked(d, HALVES if d else 1, chips, capacity, stored, slot, others, i, block)
+        block = made[0]
+        blocks[d] = [send(half, d) for half in made] if d else block
     distance = lax.rem(z - chip + chips, chips)
     first, last = (0, far), near
 
@@ -551,25 +570,30 @@
         hit = source.reshape(-1)[:, None] == jnp.arange(len(distances) * QUARTERS * capacity)[None, :]
         return jnp.tile(hit.astype(jnp.bfloat16), (1, 3))
 
-    ready = pl.pallas_call(
-        order_kernel,
-        out_shape=float_array(QUARTERS * n, columns // QUARTERS),
-        compiler_params=BIG,
-    )(*[blocks[d] for d in first], selector(first))
-    shape = blocks[near[0]].shape
+    def in_order(size, parts, selector, *ready):
+        return pl.pallas_call(
+            lambda *refs: order_kernel(len(parts), *refs),
+            out_shape=float_array(QUARTERS * n, size),
+            compiler_params=BIG,
+        )(*parts, selector, *ready)
+
+    wide = columns // QUARTERS
+    ready = in_order(wide, [blocks[d] for d in first], selector(first))
+    last = selector(last)
+    done = in_order(wide // HALVES, [blocks[d][0] for d in near], last, ready)
+    shape = blocks[near[0]][1].shape
     return pl.pallas_call(
         lambda *refs: gram_kernel(capacity == CORES * stored.shape[0], *refs),
         out_shape=(float_array(n, columns), float_array(store, n // 2 + 8, 2 * n)),
-        in_specs=[ANY, ANY, VMEM, VMEM],
+        in_specs=[ANY, ANY, VMEM, VMEM, VMEM],
         out_specs=(ANY, VMEM),
         scratch_shapes=[
             pltpu.VMEM((2, *shape), jnp.float32),
             pltpu.VMEM((n, columns), jnp.float32),
-            pltpu.VMEM((3 * n, 4 * n), jnp.int32),
             pltpu.SemaphoreType.DMA((2, QUARTERS)),
         ],
         compiler_params=BIG,
-    )(*[blocks[d] for d in last], selector(last), ready)
+    )(*[blocks[d][1] for d in near], last, done, ready)
 
 
 def per_device(stored, snap_slot):

time: 85.9 us -> 83.5 us (0.972); the launches traced: 87 us -> 83 us
  waiting for transfers between devices: 19.1 us -> 11.2 us
  Pallas kernels: 28.3 us -> 30.8 us
  starting transfers between devices: 7.84 us -> 9.76 us
    ppermute x3 -> x5, waiting for transfers between devices: 18.7 us -> 10.8 us  [send(): lax.ppermute(block, 'store', [(i, (i + d * CORES) % store) for i in range...]
    pallas_call x5 -> x6, Pallas kernels: 13.4 us -> 16.7 us  [the longest x3 8.54 us: picked(): pl.pallas_call(lambda *refs: pick_kernel(distance, (), index, halves, chi...]
    ppermute x3 -> x5, starting transfers between devices: 7.54 us -> 9.45 us  [send(): lax.ppermute(block, 'store', [(i, (i + d * CORES) % store) for i in range...]
  transfers between devices with their start and end apart: 5 -> 7, of which waited for: 3 -> 4; matrix products, arithmetic and copies ran while one was open for 5% -> 4% of each run, Pallas kernels for 12% -> 17%
where the time goes in v1:
time: 83.5 us; the launch traced here: 83 us
  Pallas kernels  30.8 us (37%)
  blocking collectives  26 us (31%)
  waiting for transfers between devices  11.2 us (13%)
  starting transfers between devices  9.76 us (12%)
  local copies, waits for them, and re-layouts  2.27 us (3%)
  between operations  1.54 us (2%)
  other arithmetic  0.98 us (1%)
    all_to_all x1, blocking collectives, per_device(): lax.all_to_all(pairs, 'rows', split_axis=0, concat_axis=0, tiled=True)  15.8 us
    ppermute x5, waiting for transfers between devices, send(): lax.ppermute(block, 'store', [(i, (i + d * CORES) % store) for i in range...  10.8 us
    all_to_all x1, blocking collectives, per_device(): lax.all_to_all(pairs, 'store', split_axis=0, concat_axis=0, tiled=True)  10.2 us
    ppermute x5, starting transfers between devices, send(): lax.ppermute(block, 'store', [(i, (i + d * CORES) % store) for i in range...  9.45 us
    pallas_call x3, Pallas kernels, picked(): pl.pallas_call(lambda *refs: pick_kernel(distance, (), index, halves, chi...  8.54 us
    pallas_call x1, Pallas kernels, per_device(): pl.pallas_call(lambda *refs: modes_kernel(columns * store * rows, *refs),...  8.28 us
    pallas_call x2, Pallas kernels, in_order(): pl.pallas_call(lambda *refs: order_kernel(len(parts), *refs), out_shape=f...  5.59 us
    pallas_call x1, Pallas kernels, relayout(): pl.pallas_call(lambda *refs: gram_kernel(capacity == CORES * stored.shape...  4.65 us
  transfers between devices with their start and end apart: 7, of which 4 were waited for; matrix products, arithmetic and copies ran while one was open for 4% of the time, Pallas kernels for 17%

profile of v1, /device:TPU:0, one launch (start us, length us, event | category | flops | bytes accessed | tf_op | source)
XLA Modules:
  0.0 83.0 jit_solution(16026613779552973823)
XLA Ops:
  0.6 0.0 copy-start.7
  0.6 1.1 %shard_map.41 = f32[16,8192]{1,0:T(8,128)S(1)} custom-call(f32[16,65536]{1,0:T(8,128)} %refs_0_.1), custom_call_target="tpu_custom_call" | custom-call | tf_op jit(solution)/shard_map/pallas_call | solution.py:604
  1.7 0.1 collective-permute-start.24
  1.8 0.0 copy-done.7
  1.8 0.2 convert_reduce_fusion
  2.0 0.6 reduce_max.9
  3.3 0.4 collective-permute-done.24
  3.7 44.8 %conditional.1 = ((f32[64,8192]{1,0:T(8,128)S(1)}, f32[8,40,128]{2,1,0:T(8,128)S(1)})) conditional(s32[]{:T(128)} %clamp.3, (f32[16,65536]{1,0:T(8,128)}, s32[1,64]{1,0:T(1,128)S(1)}, f32[16,8192]{1,0:T(8,128)S(1)}, s32[64]{0:T(128)S(1)}, s32[64]{0:T(128)S(1)}) %tuple.36, (f32[16,65536]{1,0:T(8,128)}, ...), branch_computations={%region_2.3_spmd, %region_3.4_spmd, %region_4.5_spmd, %region_5.6_... | conditional | flops 264469 | bytes 40643320 | solution.py:619
  3.7 2.5 %branch_0_fun.7 = (f32[88,2048]{1,0:T(8,128)S(1)}, f32[3,16,8192]{2,1,0:T(8,128)}) custom-call(f32[16,65536]{1,0:T(8,128)} %get-tuple-element.40.refs_0_, s32[1,64]{1,0:T(1,128)S(1)} %get-tuple-element.41.refs_1_, f32[16,8192]{1,0:T(8,128)S(1)} %get-tuple-element.42.refs_2_), custom_call_target="tpu_custom_call" | custom-call | tf_op jit(solution)/shard_map/cond/branch_0_fun/pallas_call | solution.py:369
  6.3 0.2 collective-permute-start
  6.5 4.0 %collective-permute-start.5 = (f32[88,2048]{1,0:T(8,128)S(1)}, f32[88,2048]{1,0:T(8,128)}, u32[]{:S(2)}, u32[]{:S(2)}) collective-permute-start(f32[88,2048]{1,0:T(8,128)S(1)} %get-tuple-element.44.refs_3_), channel_id=1, source_target_pairs={{0,4},{1,5},{2,6},{3,7},{4,0},{5,1},{6,2},{7,3},{8,12},{9,13},{10,... | collective-permute-start | bytes 2162696 | tf_op jit(solution)/shard_map/cond/branch_0_fun/ppermute | solution.py:391
  10.5 0.1 broadcast_add_fusion
  10.6 0.1 add.199
  10.6 0.0 copy-start
  10.7 0.0 collective-permute-done.refs_2_
  10.7 3.4 %branch_0_fun.8 = (f32[88,1024]{1,0:T(8,128)}, f32[88,1024]{1,0:T(8,128)}) custom-call(f32[16,65536]{1,0:T(8,128)} %get-tuple-element.40.refs_0_, s32[1,64]{1,0:T(1,128)S(1)} %get-tuple-element.41.refs_1_, f32[3,16,8192]{2,1,0:T(8,128)S(1)} %collective-permute-done.refs_2_, f32[88,2048]{1,0:T(8,128)S(1)} %get-tuple-element.44.refs_3_), custom_call_target="tpu_custom_call" | custom-call | tf_op jit(solution)/shard_map/cond/branch_0_fun/pallas_call | solution.py:357
  14.1 1.4 %collective-permute-start.3 = (f32[88,1024]{1,0:T(8,128)}, f32[88,1024]{1,0:T(8,128)}, u32[]{:S(2)}, u32[]{:S(2)}) collective-permute-start(f32[88,1024]{1,0:T(8,128)} %get-tuple-element.46.refs_3_), channel_id=1, source_target_pairs={{0,2},{1,3},{2,4},{3,5},{4,6},{5,7},{6,0},{7,1},{8,10},{9,11},{10,... | collective-permute-start | bytes 1081352 | tf_op jit(solution)/shard_map/cond/branch_0_fun/ppermute | solution.py:391
  15.4 0.0 copy-done
  15.5 2.6 %branch_0_fun.9 = (f32[88,1024]{1,0:T(8,128)}, f32[88,1024]{1,0:T(8,128)}) custom-call(f32[16,65536]{1,0:T(8,128)S(1)} %copy-done, s32[1,64]{1,0:T(1,128)S(1)} %get-tuple-element.41.refs_1_, f32[3,16,8192]{2,1,0:T(8,128)S(1)} %collective-permute-done.refs_2_, f32[88,1024]{1,0:T(8,128)} %get-tuple-element.46.refs_3_), custom_call_target="tpu_custom_call" | custom-call | tf_op jit(solution)/shard_map/cond/branch_0_fun/pallas_call | solution.py:357
  18.0 2.1 %collective-permute-start.4 = (f32[88,1024]{1,0:T(8,128)}, f32[88,1024]{1,0:T(8,128)}, u32[]{:S(2)}, u32[]{:S(2)}) collective-permute-start(f32[88,1024]{1,0:T(8,128)} %get-tuple-element.50.refs_3_), channel_id=1, source_target_pairs={{0,6},{1,7},{2,0},{3,1},{4,2},{5,3},{6,4},{7,5},{8,14},{9,15},{10,... | collective-permute-start | bytes 1081352 | tf_op jit(solution)/shard_map/cond/branch_0_fun/ppermute | solution.py:391
  20.1 2.0 %collective-permute-start.2 = (f32[88,1024]{1,0:T(8,128)}, f32[88,1024]{1,0:T(8,128)S(1)}, u32[]{:S(2)}, u32[]{:S(2)}) collective-permute-start(f32[88,1024]{1,0:T(8,128)} %get-tuple-element.47), channel_id=1, source_target_pairs={{0,6},{1,7},{2,0},{3,1},{4,2},{5,3},{6,4},{7,5},{8,14},{9,15},{10,... | collective-permute-start | bytes 1081352 | tf_op jit(solution)/shard_map/cond/branch_0_fun/ppermute | solution.py:391
  22.1 0.0 collective-permute-start.1
  22.2 0.2 copy.16.refs_2_
  22.4 0.1 add.193
  22.5 0.7 tile.24
  23.2 1.2 %copy.18.refs_2_ = bf16[256,528]{1,0:T(8,128)(2,1)S(1)} copy(bf16[256,528]{0,1:T(8,128)(2,1)} %bitcast.16) | data formatting | bytes 540672 | tf_op jit(solution)/shard_map/cond/branch_0_fun/tile | solution.py:571
  24.4 2.6 %branch_0_fun.10.refs_0_ = f32[88,2048]{1,0:T(8,128)S(1)} custom-call(f32[16,65536]{1,0:T(8,128)} %get-tuple-element.40.refs_0_, s32[1,64]{1,0:T(1,128)S(1)} %get-tuple-element.41.refs_1_, f32[3,16,8192]{2,1,0:T(8,128)S(1)} %collective-permute-done.refs_2_, f32[88,1024]{1,0:T(8,128)} %get-tuple-element.50.refs_3_), custom_call_target="tpu_custom_call" | custom-call | tf_op jit(solution)/shard_map/cond/branch_0_fun/pallas_call | solution.py:357
  26.9 0.6 collective-permute-done.5.refs_1_
  27.6 3.4 %branch_0_fun.11.refs_3_.refs_4_ = f32[256,2048]{1,0:T(8,128)S(1)} custom-call(f32[88,2048]{1,0:T(8,128)S(1)} %branch_0_fun.10.refs_0_, f32[88,2048]{1,0:T(8,128)} %collective-permute-done.5.refs_1_, bf16[256,528]{1,0:T(8,128)(2,1)S(1)} %copy.16.refs_2_), custom_call_target="tpu_custom_call" | custom-call | tf_op jit(solution)/shard_map/cond/branch_0_fun/pallas_call | solution.py:574
  30.9 5.3 %collective-permute-done.4.refs_1_ = f32[88,1024]{1,0:T(8,128)} collective-permute-done((f32[88,1024]{1,0:T(8,128)}, f32[88,1024]{1,0:T(8,128)}, u32[]{:S(2)}, u32[]{:S(2)}) %collective-permute-start.4) | collective-permute-done | bytes 360480 | tf_op jit(solution)/shard_map/cond/branch_0_fun/ppermute | solution.py:391
  36.3 0.0 collective-permute-done.3.refs_0_
  36.3 2.2 %branch_0_fun.12.refs_3_ = f32[256,1024]{1,0:T(8,128)S(1)} custom-call(f32[88,1024]{1,0:T(8,128)} %collective-permute-done.3.refs_0_, f32[88,1024]{1,0:T(8,128)} %collective-permute-done.4.refs_1_, bf16[256,528]{1,0:T(8,128)(2,1)S(1)} %copy.18.refs_2_, f32[256,2048]{1,0:T(8,128)S(1)} %branch_0_fun.11.refs_3_.refs_4_), custom_call_target="tpu_custom_call" | custom-call | tf_op jit(solution)/shard_map/cond/branch_0_fun/pallas_call | solution.py:574
  38.5 4.8 %collective-permute-done.2.refs_1_ = f32[88,1024]{1,0:T(8,128)S(1)} collective-permute-done((f32[88,1024]{1,0:T(8,128)}, f32[88,1024]{1,0:T(8,128)S(1)}, u32[]{:S(2)}, u32[]{:S(2)}) %collective-permute-start.2) | collective-permute-done | bytes 360480 | tf_op jit(solution)/shard_map/cond/branch_0_fun/ppermute | solution.py:391
  43.3 0.0 collective-permute-done.1.refs_0_
  43.3 4.7 %branch_0_fun.13 = (f32[64,8192]{1,0:T(8,128)S(1)}, f32[8,40,128]{2,1,0:T(8,128)S(1)}) custom-call(f32[88,1024]{1,0:T(8,128)} %collective-permute-done.1.refs_0_, f32[88,1024]{1,0:T(8,128)S(1)} %collective-permute-done.2.refs_1_, bf16[256,528]{1,0:T(8,128)(2,1)S(1)} %copy.18.refs_2_, f32[256,1024]{1,0:T(8,128)S(1)} %branch_0_fun.12.refs_3_, ...), custom_call_target="tpu_custom_call" | custom-call | tf_op jit(solution)/shard_map/cond/branch_0_fun/pallas_call | solution.py:585
  48.5 10.2 %all_to_all.10.in_ref = f32[8,40,128]{2,1,0:T(8,128)S(1)} all-to-all(f32[8,40,128]{2,1,0:T(8,128)S(1)} %get-tuple-element.88), channel_id=1, replica_groups=mesh['rows'=16,'store'=8] {'store'}, dimensions={0} | all-to-all | bytes 327680 | tf_op jit(solution)/shard_map/all_to_all | solution.py:621
  58.7 0.1 shard_map.42
  58.8 15.8 %all_to_all.11.refs_0_ = f32[16,40,128]{2,1,0:T(8,128)S(1)} all-to-all(f32[16,40,128]{2,1,0:T(8,128)S(1)} %shard_map.42), channel_id=1, replica_groups=mesh['rows'=16,'store'=8] {'rows'}, dimensions={0} | all-to-all | bytes 655360 | tf_op jit(solution)/shard_map/all_to_all | solution.py:623
  74.6 8.3 %shard_map.43 = (f32[64,8192]{1,0:T(8,128)}, f32[64,64]{1,0:T(8,128)}) custom-call(f32[16,40,128]{2,1,0:T(8,128)S(1)} %all_to_all.11.refs_0_, f32[64,8192]{1,0:T(8,128)S(1)} %get-tuple-element.89.refs_1_), custom_call_target="tpu_custom_call" | custom-call | tf_op jit(solution)/shard_map/pallas_call | solution.py:624
  (7 shorter events, 0.1 us)
Async XLA Ops:
  0.6 1.2 %copy-start.7 = (s32[64]{0:T(128)S(1)}, s32[64]{0:T(128)}, u32[]{:S(2)}) copy-start(s32[64]{0:T(128)} %param.7) | copy-start | bytes 772
  1.7 2.0 %collective-permute-start.24 = (f32[16,8192]{1,0:T(8,128)S(1)}, f32[16,8192]{1,0:T(8,128)S(1)}, u32[]{:S(2)}, u32[]{:S(2)}) collective-permute-start(f32[16,8192]{1,0:T(8,128)S(1)} %shard_map.41), channel_id=1, source_target_pairs={{0,1},{1,0},{2,3},{3,2},{4,5},{5,4},{6,7},{7,6},{8,9},{9,8},{10,11... | collective-permute-start | bytes 1572872 | tf_op jit(solution)/shard_map/ppermute | solution.py:386
  6.3 4.4 %collective-permute-start = (f32[3,16,8192]{2,1,0:T(8,128)}, f32[3,16,8192]{2,1,0:T(8,128)S(1)}, u32[]{:S(2)}, u32[]{:S(2)}) collective-permute-start(f32[3,16,8192]{2,1,0:T(8,128)} %get-tuple-element.43), channel_id=1, source_target_pairs={{0,1},{1,0},{2,3},{3,2},{4,5},{5,4},{6,7},{7,6},{8,9},{9,8},{10,11... | collective-permute-start | bytes 4718600 | tf_op jit(solution)/shard_map/cond/branch_0_fun/ppermute | solution.py:386
  6.5 21.1 %collective-permute-start.5 = (f32[88,2048]{1,0:T(8,128)S(1)}, f32[88,2048]{1,0:T(8,128)}, u32[]{:S(2)}, u32[]{:S(2)}) collective-permute-start(f32[88,2048]{1,0:T(8,128)S(1)} %get-tuple-element.44.refs_3_), channel_id=1, source_target_pairs={{0,4},{1,5},{2,6},{3,7},{4,0},{5,1},{6,2},{7,3},{8,12},{9,13},{10,... | collective-permute-start | bytes 2162696 | tf_op jit(solution)/shard_map/cond/branch_0_fun/ppermute | solution.py:391
  10.6 4.8 %copy-start = (f32[16,65536]{1,0:T(8,128)S(1)}, f32[16,65536]{1,0:T(8,128)}, u32[]{:S(2)}) copy-start(f32[16,65536]{1,0:T(8,128)} %get-tuple-element.40.refs_0_) | copy-start | bytes 12582916 | tf_op jit(solution)/shard_map/cond
  14.1 22.2 %collective-permute-start.3 = (f32[88,1024]{1,0:T(8,128)}, f32[88,1024]{1,0:T(8,128)}, u32[]{:S(2)}, u32[]{:S(2)}) collective-permute-start(f32[88,1024]{1,0:T(8,128)} %get-tuple-element.46.refs_3_), channel_id=1, source_target_pairs={{0,2},{1,3},{2,4},{3,5},{4,6},{5,7},{6,0},{7,1},{8,10},{9,11},{10,... | collective-permute-start | bytes 1081352 | tf_op jit(solution)/shard_map/cond/branch_0_fun/ppermute | solution.py:391
  18.0 18.3 %collective-permute-start.4 = (f32[88,1024]{1,0:T(8,128)}, f32[88,1024]{1,0:T(8,128)}, u32[]{:S(2)}, u32[]{:S(2)}) collective-permute-start(f32[88,1024]{1,0:T(8,128)} %get-tuple-element.50.refs_3_), channel_id=1, source_target_pairs={{0,6},{1,7},{2,0},{3,1},{4,2},{5,3},{6,4},{7,5},{8,14},{9,15},{10,... | collective-permute-start | bytes 1081352 | tf_op jit(solution)/shard_map/cond/branch_0_fun/ppermute | solution.py:391
  20.1 23.2 %collective-permute-start.2 = (f32[88,1024]{1,0:T(8,128)}, f32[88,1024]{1,0:T(8,128)S(1)}, u32[]{:S(2)}, u32[]{:S(2)}) collective-permute-start(f32[88,1024]{1,0:T(8,128)} %get-tuple-element.47), channel_id=1, source_target_pairs={{0,6},{1,7},{2,0},{3,1},{4,2},{5,3},{6,4},{7,5},{8,14},{9,15},{10,... | collective-permute-start | bytes 1081352 | tf_op jit(solution)/shard_map/cond/branch_0_fun/ppermute | solution.py:391
  22.1 21.2 %collective-permute-start.1 = (f32[88,1024]{1,0:T(8,128)}, f32[88,1024]{1,0:T(8,128)}, u32[]{:S(2)}, u32[]{:S(2)}) collective-permute-start(f32[88,1024]{1,0:T(8,128)} %get-tuple-element.45), channel_id=1, source_target_pairs={{0,2},{1,3},{2,4},{3,5},{4,6},{5,7},{6,0},{7,1},{8,10},{9,11},{10,... | collective-permute-start | bytes 1081352 | tf_op jit(solution)/shard_map/cond/branch_0_fun/ppermute | solution.py:391

commit v2 on v1

--- a/solution.py
+++ b/solution.py
@@ -378,7 +378,7 @@
             pltpu.VMEM((QUARTERS * capacity, columns // QUARTERS), jnp.float32),
             pltpu.SemaphoreType.DMA((2 + count,)),
         ],
-        compiler_params=pltpu.CompilerParams(vmem_limit_bytes=5 * 2**20),
+        compiler_params=pltpu.CompilerParams(vmem_limit_bytes=56 * 2**20),
     )(stored, slot, other)
 
 

time: 83.5 us -> 85.3 us (1.022); the launches traced: 83 us -> 86.3 us
  waiting for transfers between devices: 11.2 us -> 13.9 us
  local copies, waits for them, and re-layouts: 2.27 us -> 3.41 us
    ppermute x5, waiting for transfers between devices: 10.8 us -> 13.5 us  [send(): lax.ppermute(block, 'store', [(i, (i + d * CORES) % store) for i in range...]
    cond x2 -> x4, local copies, waits for them, and re-layouts: 0.01 us -> 1.14 us
    pallas_call x2, Pallas kernels: 5.59 us -> 4.48 us  [in_order(): pl.pallas_call(lambda *refs: order_kernel(len(parts), *refs), out_shape=f...]
  transfers between devices with their start and end apart: 7 -> 7, of which waited for: 4 -> 4; matrix products, arithmetic and copies ran while one was open for 4% -> 4% of each run, Pallas kernels for 17% -> 15%
where the time goes in v2:
time: 85.3 us; the launch traced here: 86.3 us
  Pallas kernels  30 us (35%)
  blocking collectives  26 us (30%)
  waiting for transfers between devices  13.9 us (16%)
  starting transfers between devices  9.91 us (12%)
  local copies, waits for them, and re-layouts  3.41 us (4%)
  between operations  1.54 us (2%)
  other arithmetic  0.98 us (1%)
    all_to_all x1, blocking collectives, per_device(): lax.all_to_all(pairs, 'rows', split_axis=0, concat_axis=0, tiled=True)  15.8 us
    ppermute x5, waiting for transfers between devices, send(): lax.ppermute(block, 'store', [(i, (i + d * CORES) % store) for i in range...  13.5 us
    all_to_all x1, blocking collectives, per_device(): lax.all_to_all(pairs, 'store', split_axis=0, concat_axis=0, tiled=True)  10.2 us
    ppermute x5, starting transfers between devices, send(): lax.ppermute(block, 'store', [(i, (i + d * CORES) % store) for i in range...  9.59 us
    pallas_call x3, Pallas kernels, picked(): pl.pallas_call(lambda *refs: pick_kernel(distance, (), index, halves, chi...  8.61 us
    pallas_call x1, Pallas kernels, per_device(): pl.pallas_call(lambda *refs: modes_kernel(columns * store * rows, *refs),...  8.28 us
    pallas_call x1, Pallas kernels, relayout(): pl.pallas_call(lambda *refs: gram_kernel(capacity == CORES * stored.shape...  4.68 us
    pallas_call x2, Pallas kernels, in_order(): pl.pallas_call(lambda *refs: order_kernel(len(parts), *refs), out_shape=f...  4.48 us
  transfers between devices with their start and end apart: 7, of which 4 were waited for; matrix products, arithmetic and copies ran while one was open for 4% of the time, Pallas kernels for 15%

profile of v2, /device:TPU:0, one launch (start us, length us, event | category | flops | bytes accessed | tf_op | source)
XLA Modules:
  0.0 86.3 jit_solution(17227636248331527234)
XLA Ops:
  0.6 0.0 copy-start.8
  0.6 1.1 %shard_map.41 = f32[16,8192]{1,0:T(8,128)S(1)} custom-call(f32[16,65536]{1,0:T(8,128)} %refs_0_.1), custom_call_target="tpu_custom_call" | custom-call | tf_op jit(solution)/shard_map/pallas_call | solution.py:604
  1.7 0.1 collective-permute-start.24
  1.8 0.0 copy-done.8
  1.8 0.2 convert_reduce_fusion
  2.0 0.6 reduce_max.9
  3.3 0.4 collective-permute-done.24
  3.7 48.1 %conditional.1 = ((f32[64,8192]{1,0:T(8,128)S(1)}, f32[8,40,128]{2,1,0:T(8,128)S(1)})) conditional(s32[]{:T(128)} %clamp.3, (f32[16,65536]{1,0:T(8,128)}, s32[1,64]{1,0:T(1,128)S(1)}, f32[16,8192]{1,0:T(8,128)S(1)}, s32[64]{0:T(128)S(1)}, s32[64]{0:T(128)S(1)}) %tuple.36, (f32[16,65536]{1,0:T(8,128)}, ...), branch_computations={%region_2.3_spmd, %region_3.4_spmd, %region_4.5_spmd, %region_5.6_... | conditional | flops 264469 | bytes 42740472 | solution.py:619
  3.7 2.8 %branch_1_fun.7 = (f32[96,2048]{1,0:T(8,128)}, f32[3,16,8192]{2,1,0:T(8,128)}) custom-call(f32[16,65536]{1,0:T(8,128)} %get-tuple-element.51.refs_0_, s32[1,64]{1,0:T(1,128)S(1)} %get-tuple-element.52.refs_1_, f32[16,8192]{1,0:T(8,128)S(1)} %get-tuple-element.53.refs_2_), custom_call_target="tpu_custom_call" | custom-call | tf_op jit(solution)/shard_map/cond/branch_1_fun/pallas_call | solution.py:369
  6.5 0.2 collective-permute-start.6
  6.7 4.0 %collective-permute-start.11 = (f32[96,2048]{1,0:T(8,128)}, f32[96,2048]{1,0:T(8,128)S(1)}, u32[]{:S(2)}, u32[]{:S(2)}) collective-permute-start(f32[96,2048]{1,0:T(8,128)} %get-tuple-element.55.refs_3_), channel_id=1, source_target_pairs={{0,4},{1,5},{2,6},{3,7},{4,0},{5,1},{6,2},{7,3},{8,12},{9,13},{10,... | collective-permute-start | bytes 2359304 | tf_op jit(solution)/shard_map/cond/branch_1_fun/ppermute | solution.py:391
  10.8 0.1 broadcast_add_fusion.2
  10.8 0.1 add.212
  10.9 0.0 collective-permute-done.6.refs_2_
  10.9 0.0 copy-start.2
  10.9 1.1 %copy-done.2 = f32[96,2048]{1,0:T(8,128)S(1)} copy-done((f32[96,2048]{1,0:T(8,128)S(1)}, f32[96,2048]{1,0:T(8,128)}, u32[]{:S(2)}) %copy-start.2) | copy-done | bytes 786456 | tf_op jit(solution)/shard_map/cond
  12.0 0.0 copy-start.5
  12.0 3.5 %branch_1_fun.8 = (f32[96,1024]{1,0:T(8,128)}, f32[96,1024]{1,0:T(8,128)}) custom-call(f32[16,65536]{1,0:T(8,128)} %get-tuple-element.51.refs_0_, s32[1,64]{1,0:T(1,128)S(1)} %get-tuple-element.52.refs_1_, f32[3,16,8192]{2,1,0:T(8,128)S(1)} %collective-permute-done.6.refs_2_, f32[96,2048]{1,0:T(8,128)S(1)} %copy-done.2), custom_call_target="tpu_custom_call" | custom-call | tf_op jit(solution)/shard_map/cond/branch_1_fun/pallas_call | solution.py:357
  15.5 1.4 %collective-permute-start.9 = (f32[96,1024]{1,0:T(8,128)}, f32[96,1024]{1,0:T(8,128)}, u32[]{:S(2)}, u32[]{:S(2)}) collective-permute-start(f32[96,1024]{1,0:T(8,128)} %get-tuple-element.57.refs_3_), channel_id=1, source_target_pairs={{0,2},{1,3},{2,4},{3,5},{4,6},{5,7},{6,0},{7,1},{8,10},{9,11},{10,... | collective-permute-start | bytes 1179656 | tf_op jit(solution)/shard_map/cond/branch_1_fun/ppermute | solution.py:391
  16.9 0.0 copy-done.5
  16.9 2.6 %branch_1_fun.9 = (f32[96,1024]{1,0:T(8,128)}, f32[96,1024]{1,0:T(8,128)}) custom-call(f32[16,65536]{1,0:T(8,128)S(1)} %copy-done.5, s32[1,64]{1,0:T(1,128)S(1)} %get-tuple-element.52.refs_1_, f32[3,16,8192]{2,1,0:T(8,128)S(1)} %collective-permute-done.6.refs_2_, f32[96,1024]{1,0:T(8,128)} %get-tuple-element.57.refs_3_), custom_call_target="tpu_custom_call" | custom-call | tf_op jit(solution)/shard_map/cond/branch_1_fun/pallas_call | solution.py:357
  19.5 2.2 %collective-permute-start.10 = (f32[96,1024]{1,0:T(8,128)}, f32[96,1024]{1,0:T(8,128)}, u32[]{:S(2)}, u32[]{:S(2)}) collective-permute-start(f32[96,1024]{1,0:T(8,128)} %get-tuple-element.61.refs_3_), channel_id=1, source_target_pairs={{0,6},{1,7},{2,0},{3,1},{4,2},{5,3},{6,4},{7,5},{8,14},{9,15},{10,... | collective-permute-start | bytes 1179656 | tf_op jit(solution)/shard_map/cond/branch_1_fun/ppermute | solution.py:391
  21.7 2.0 %collective-permute-start.8 = (f32[96,1024]{1,0:T(8,128)}, f32[96,1024]{1,0:T(8,128)S(1)}, u32[]{:S(2)}, u32[]{:S(2)}) collective-permute-start(f32[96,1024]{1,0:T(8,128)} %get-tuple-element.58), channel_id=1, source_target_pairs={{0,6},{1,7},{2,0},{3,1},{4,2},{5,3},{6,4},{7,5},{8,14},{9,15},{10,... | collective-permute-start | bytes 1179656 | tf_op jit(solution)/shard_map/cond/branch_1_fun/ppermute | solution.py:391
  23.7 0.0 collective-permute-start.7
  23.8 0.2 copy.19.refs_2_
  24.0 0.1 add.206
  24.1 0.7 tile.40
  24.8 1.2 %copy.21.refs_2_ = bf16[256,576]{1,0:T(8,128)(2,1)S(1)} copy(bf16[256,576]{0,1:T(8,128)(2,1)} %bitcast.14) | data formatting | bytes 589824 | tf_op jit(solution)/shard_map/cond/branch_1_fun/tile | solution.py:571
  26.0 2.6 %branch_1_fun.10.refs_0_ = f32[96,2048]{1,0:T(8,128)S(1)} custom-call(f32[16,65536]{1,0:T(8,128)} %get-tuple-element.51.refs_0_, s32[1,64]{1,0:T(1,128)S(1)} %get-tuple-element.52.refs_1_, f32[3,16,8192]{2,1,0:T(8,128)S(1)} %collective-permute-done.6.refs_2_, f32[96,1024]{1,0:T(8,128)} %get-tuple-element.61.refs_3_), custom_call_target="tpu_custom_call" | custom-call | tf_op jit(solution)/shard_map/cond/branch_1_fun/pallas_call | solution.py:357
  28.6 0.8 collective-permute-done.11.refs_1_
  29.3 2.2 %branch_1_fun.11.refs_3_.refs_4_ = f32[256,2048]{1,0:T(8,128)S(1)} custom-call(f32[96,2048]{1,0:T(8,128)S(1)} %branch_1_fun.10.refs_0_, f32[96,2048]{1,0:T(8,128)S(1)} %collective-permute-done.11.refs_1_, bf16[256,576]{1,0:T(8,128)(2,1)S(1)} %copy.19.refs_2_), custom_call_target="tpu_custom_call" | custom-call | tf_op jit(solution)/shard_map/cond/branch_1_fun/pallas_call | solution.py:574
  31.6 7.2 %collective-permute-done.10.refs_1_ = f32[96,1024]{1,0:T(8,128)} collective-permute-done((f32[96,1024]{1,0:T(8,128)}, f32[96,1024]{1,0:T(8,128)}, u32[]{:S(2)}, u32[]{:S(2)}) %collective-permute-start.10) | collective-permute-done | bytes 393248 | tf_op jit(solution)/shard_map/cond/branch_1_fun/ppermute | solution.py:391
  38.8 0.0 collective-permute-done.9.refs_0_
  38.8 2.2 %branch_1_fun.12.refs_3_ = f32[256,1024]{1,0:T(8,128)S(1)} custom-call(f32[96,1024]{1,0:T(8,128)} %collective-permute-done.9.refs_0_, f32[96,1024]{1,0:T(8,128)} %collective-permute-done.10.refs_1_, bf16[256,576]{1,0:T(8,128)(2,1)S(1)} %copy.21.refs_2_, f32[256,2048]{1,0:T(8,128)S(1)} %branch_1_fun.11.refs_3_.refs_4_), custom_call_target="tpu_custom_call" | custom-call | tf_op jit(solution)/shard_map/cond/branch_1_fun/pallas_call | solution.py:574
  41.1 5.5 %collective-permute-done.8.refs_1_ = f32[96,1024]{1,0:T(8,128)S(1)} collective-permute-done((f32[96,1024]{1,0:T(8,128)}, f32[96,1024]{1,0:T(8,128)S(1)}, u32[]{:S(2)}, u32[]{:S(2)}) %collective-permute-start.8) | collective-permute-done | bytes 393248 | tf_op jit(solution)/shard_map/cond/branch_1_fun/ppermute | solution.py:391
  46.6 0.0 collective-permute-done.7.refs_0_
  46.6 4.7 %branch_1_fun.13 = (f32[64,8192]{1,0:T(8,128)S(1)}, f32[8,40,128]{2,1,0:T(8,128)S(1)}) custom-call(f32[96,1024]{1,0:T(8,128)} %collective-permute-done.7.refs_0_, f32[96,1024]{1,0:T(8,128)S(1)} %collective-permute-done.8.refs_1_, bf16[256,576]{1,0:T(8,128)(2,1)S(1)} %copy.21.refs_2_, f32[256,1024]{1,0:T(8,128)S(1)} %branch_1_fun.12.refs_3_, ...), custom_call_target="tpu_custom_call" | custom-call | tf_op jit(solution)/shard_map/cond/branch_1_fun/pallas_call | solution.py:585
  51.8 10.2 %all_to_all.10.in_ref = f32[8,40,128]{2,1,0:T(8,128)S(1)} all-to-all(f32[8,40,128]{2,1,0:T(8,128)S(1)} %get-tuple-element.88), channel_id=1, replica_groups=mesh['rows'=16,'store'=8] {'store'}, dimensions={0} | all-to-all | bytes 327680 | tf_op jit(solution)/shard_map/all_to_all | solution.py:621
  62.0 0.1 shard_map.42
  62.1 15.8 %all_to_all.11.refs_0_ = f32[16,40,128]{2,1,0:T(8,128)S(1)} all-to-all(f32[16,40,128]{2,1,0:T(8,128)S(1)} %shard_map.42), channel_id=1, replica_groups=mesh['rows'=16,'store'=8] {'rows'}, dimensions={0} | all-to-all | bytes 655360 | tf_op jit(solution)/shard_map/all_to_all | solution.py:623
  77.8 8.3 %shard_map.43 = (f32[64,8192]{1,0:T(8,128)}, f32[64,64]{1,0:T(8,128)}) custom-call(f32[16,40,128]{2,1,0:T(8,128)S(1)} %all_to_all.11.refs_0_, f32[64,8192]{1,0:T(8,128)S(1)} %get-tuple-element.89.refs_1_), custom_call_target="tpu_custom_call" | custom-call | tf_op jit(solution)/shard_map/pallas_call | solution.py:624
  (7 shorter events, 0.1 us)
Async XLA Ops:
  0.6 1.2 %copy-start.8 = (s32[64]{0:T(128)S(1)}, s32[64]{0:T(128)}, u32[]{:S(2)}) copy-start(s32[64]{0:T(128)} %param.7) | copy-start | bytes 772
  1.7 2.0 %collective-permute-start.24 = (f32[16,8192]{1,0:T(8,128)S(1)}, f32[16,8192]{1,0:T(8,128)S(1)}, u32[]{:S(2)}, u32[]{:S(2)}) collective-permute-start(f32[16,8192]{1,0:T(8,128)S(1)} %shard_map.41), channel_id=1, source_target_pairs={{0,1},{1,0},{2,3},{3,2},{4,5},{5,4},{6,7},{7,6},{8,9},{9,8},{10,11... | collective-permute-start | bytes 1572872 | tf_op jit(solution)/shard_map/ppermute | solution.py:386
  6.5 4.4 %collective-permute-start.6 = (f32[3,16,8192]{2,1,0:T(8,128)}, f32[3,16,8192]{2,1,0:T(8,128)S(1)}, u32[]{:S(2)}, u32[]{:S(2)}) collective-permute-start(f32[3,16,8192]{2,1,0:T(8,128)} %get-tuple-element.54), channel_id=1, source_target_pairs={{0,1},{1,0},{2,3},{3,2},{4,5},{5,4},{6,7},{7,6},{8,9},{9,8},{10,11... | collective-permute-start | bytes 4718600 | tf_op jit(solution)/shard_map/cond/branch_1_fun/ppermute | solution.py:386
  6.7 22.6 %collective-permute-start.11 = (f32[96,2048]{1,0:T(8,128)}, f32[96,2048]{1,0:T(8,128)S(1)}, u32[]{:S(2)}, u32[]{:S(2)}) collective-permute-start(f32[96,2048]{1,0:T(8,128)} %get-tuple-element.55.refs_3_), channel_id=1, source_target_pairs={{0,4},{1,5},{2,6},{3,7},{4,0},{5,1},{6,2},{7,3},{8,12},{9,13},{10,... | collective-permute-start | bytes 2359304 | tf_op jit(solution)/shard_map/cond/branch_1_fun/ppermute | solution.py:391
  10.9 1.1 %copy-start.2 = (f32[96,2048]{1,0:T(8,128)S(1)}, f32[96,2048]{1,0:T(8,128)}, u32[]{:S(2)}) copy-start(f32[96,2048]{1,0:T(8,128)} %get-tuple-element.55.refs_3_) | copy-start | bytes 2359300 | tf_op jit(solution)/shard_map/cond
  12.0 4.8 %copy-start.5 = (f32[16,65536]{1,0:T(8,128)S(1)}, f32[16,65536]{1,0:T(8,128)}, u32[]{:S(2)}) copy-start(f32[16,65536]{1,0:T(8,128)} %get-tuple-element.51.refs_0_) | copy-start | bytes 12582916 | tf_op jit(solution)/shard_map/cond
  15.5 23.3 %collective-permute-start.9 = (f32[96,1024]{1,0:T(8,128)}, f32[96,1024]{1,0:T(8,128)}, u32[]{:S(2)}, u32[]{:S(2)}) collective-permute-start(f32[96,1024]{1,0:T(8,128)} %get-tuple-element.57.refs_3_), channel_id=1, source_target_pairs={{0,2},{1,3},{2,4},{3,5},{4,6},{5,7},{6,0},{7,1},{8,10},{9,11},{10,... | collective-permute-start | bytes 1179656 | tf_op jit(solution)/shard_map/cond/branch_1_fun/ppermute | solution.py:391
  19.5 19.4 %collective-permute-start.10 = (f32[96,1024]{1,0:T(8,128)}, f32[96,1024]{1,0:T(8,128)}, u32[]{:S(2)}, u32[]{:S(2)}) collective-permute-start(f32[96,1024]{1,0:T(8,128)} %get-tuple-element.61.refs_3_), channel_id=1, source_target_pairs={{0,6},{1,7},{2,0},{3,1},{4,2},{5,3},{6,4},{7,5},{8,14},{9,15},{10,... | collective-permute-start | bytes 1179656 | tf_op jit(solution)/shard_map/cond/branch_1_fun/ppermute | solution.py:391
  21.7 24.9 %collective-permute-start.8 = (f32[96,1024]{1,0:T(8,128)}, f32[96,1024]{1,0:T(8,128)S(1)}, u32[]{:S(2)}, u32[]{:S(2)}) collective-permute-start(f32[96,1024]{1,0:T(8,128)} %get-tuple-element.58), channel_id=1, source_target_pairs={{0,6},{1,7},{2,0},{3,1},{4,2},{5,3},{6,4},{7,5},{8,14},{9,15},{10,... | collective-permute-start | bytes 1179656 | tf_op jit(solution)/shard_map/cond/branch_1_fun/ppermute | solution.py:391
  23.7 22.9 %collective-permute-start.7 = (f32[96,1024]{1,0:T(8,128)}, f32[96,1024]{1,0:T(8,128)}, u32[]{:S(2)}, u32[]{:S(2)}) collective-permute-start(f32[96,1024]{1,0:T(8,128)} %get-tuple-element.56), channel_id=1, source_target_pairs={{0,2},{1,3},{2,4},{3,5},{4,6},{5,7},{6,0},{7,1},{8,10},{9,11},{10,... | collective-permute-start | bytes 1179656 | tf_op jit(solution)/shard_map/cond/branch_1_fun/ppermute | solution.py:391
